TPU v7x, 512 devices: a whole 4x4x16 slice. The times are simulated.
512 devices in a mesh: fsdp: 8 (over y_hi, x), shard: 64 (over y_lo, z, core).
Axes of the slice: x: 4, y: 4 (y_hi: 2, y_lo: 2; y = y_hi * 2 + y_lo), z: 16, core: 2. Of those that a mesh axis runs over, the one named last changes fastest.
Arguments:
- query_momentum: float32 [256, 294912], P('fsdp', 'shard')
- key_value_momentum: float32 [256, 131072], P('fsdp', 'shard')
- query_blocks: bfloat16 [256, 294912], P('fsdp', 'shard'), may hold values from -6 to 6
- key_value_blocks: bfloat16 [256, 131072], P('fsdp', 'shard'), may hold values from -6 to 6
- clip_flags: int32 [256], P('fsdp'), may hold values 0 or 1
- logit_max: float32 [256], P('fsdp'), may hold values from 25 to 400
Outputs:
- q_updated: bfloat16 [256, 294912], P(None, 'shard')
- kv_updated: bfloat16 [256, 131072], P(None, 'shard')
All inputs are finite; a program needn't handle non-finite values. No bound on the sum of `clip_flags` on one device may be relied on, other than what follows from the above.
Results may differ from a plain program's by a relative error of at most 0.004.
Values may be sent and summed in bfloat16 or wider, within the bound.
A program may use at most 64 MiB of HBM per device.

v0:
```python
import math

import jax
import jax.numpy as jnp
from jax import lax
from jax.sharding import PartitionSpec as P

PLAIN_FEATURES = 128
ROTARY_FEATURES = 64
VALUE_FEATURES = 128
QUERY_RANK = 1536
KEY_VALUE_RANK = 512
NS_ITERS = 5


COEF_A = 3.4445
COEF_B = -4.775
COEF_C = 2.0315
CLIP_TAU = 100.0
LEARNING_RATE = 0.5
DECAY_WEIGHT = 0.1


def make_orthogonal(matrix):
    frobenius = jnp.sqrt(jnp.sum(matrix * matrix))
    iterate = matrix / (frobenius + 1e-07)
    for sweep in range(NS_ITERS):
        gram_matrix = jnp.dot(iterate, iterate.T, precision=lax.Precision.HIGHEST)
        polynomial = COEF_B * gram_matrix + COEF_C * jnp.dot(
            gram_matrix, gram_matrix, precision=lax.Precision.HIGHEST
        )
        iterate = COEF_A * iterate + jnp.dot(polynomial, iterate, precision=lax.Precision.HIGHEST)
    return iterate.astype(jnp.bfloat16)


def per_device(
    query_momentum, key_value_momentum, query_blocks, key_value_blocks, clip_flags, logit_max
):
    holder_devices = lax.axis_size("shard")
    half_axis = query_momentum.shape[0]
    query_columns = query_momentum.shape[1]
    key_value_columns = key_value_momentum.shape[1]
    location = lax.axis_index("shard")
    query_row_list = PLAIN_FEATURES + ROTARY_FEATURES
    key_value_row_list = PLAIN_FEATURES + VALUE_FEATURES

    def query_job(fragments):
        return make_orthogonal(fragments.reshape(query_row_list, QUERY_RANK)).reshape(
            holder_devices, query_columns
        )

    def keyval_job(fragments):
        return make_orthogonal(fragments.reshape(key_value_row_list, KEY_VALUE_RANK)).reshape(
            holder_devices, key_value_columns
        )

    query_send = jnp.concatenate([query_momentum, jnp.zeros_like(query_momentum)], 0)
    keyval_send = jnp.concatenate([jnp.zeros_like(key_value_momentum), key_value_momentum], 0)
    query_recv, keyval_recv = (
        lax.all_to_all(
            query_send.astype(jnp.bfloat16), "shard", split_axis=0, concat_axis=0, tiled=True
        ).astype(query_send.dtype),
        lax.all_to_all(
            keyval_send.astype(jnp.bfloat16), "shard", split_axis=0, concat_axis=0, tiled=True
        ).astype(keyval_send.dtype),
    )

    def query_branch(operands):
        return (
            query_job(operands[0]),
            jnp.zeros((holder_devices, key_value_columns), jnp.bfloat16),
        )

    def keyval_branch(operands):
        return (jnp.zeros((holder_devices, query_columns), jnp.bfloat16), keyval_job(operands[1]))

    query_done, keyval_done = lax.cond(
        location < half_axis, query_branch, keyval_branch, (query_recv, keyval_recv)
    )
    query_back, keyval_back = (
        lax.all_to_all(query_done, "shard", split_axis=0, concat_axis=0, tiled=True),
        lax.all_to_all(keyval_done, "shard", split_axis=0, concat_axis=0, tiled=True),
    )
    query_update_step = query_back[:half_axis]
    key_value_update = keyval_back[half_axis:]
    eta = jnp.where(
        clip_flags > 0, jnp.minimum(jnp.float32(1.0), CLIP_TAU / logit_max), jnp.float32(1.0)
    )
    root = jnp.sqrt(eta)
    query_single_row = (
        location * query_columns + jnp.arange(query_columns, dtype=jnp.int32)
    ) // QUERY_RANK
    key_value_single_row = (
        location * key_value_columns + jnp.arange(key_value_columns, dtype=jnp.int32)
    ) // KEY_VALUE_RANK
    query_scale_factor = jnp.where(
        query_single_row[None, :] < PLAIN_FEATURES, root[:, None], eta[:, None]
    )
    key_value_scale = jnp.where(
        key_value_single_row[None, :] < PLAIN_FEATURES, root[:, None], jnp.float32(1.0)
    )
    query_fresh = query_scale_factor * (
        query_blocks.astype(jnp.float32) * (1.0 - LEARNING_RATE * DECAY_WEIGHT)
        - LEARNING_RATE * 0.2 * math.sqrt(QUERY_RANK) * query_update_step.astype(jnp.float32)
    )
    key_value_fresh = key_value_scale * (
        key_value_blocks.astype(jnp.float32) * (1.0 - LEARNING_RATE * DECAY_WEIGHT)
        - LEARNING_RATE * 0.2 * math.sqrt(KEY_VALUE_RANK) * key_value_update.astype(jnp.float32)
    )
    query_all, keyval_all = (
        lax.all_gather(query_fresh.astype(jnp.bfloat16), "fsdp", axis=0, tiled=True),
        lax.all_gather(key_value_fresh.astype(jnp.bfloat16), "fsdp", axis=0, tiled=True),
    )
    return (query_all, keyval_all)


def solution(mesh):
    placed = (
        P("fsdp", "shard"),
        P("fsdp", "shard"),
        P("fsdp", "shard"),
        P("fsdp", "shard"),
        P("fsdp"),
        P("fsdp"),
    )
    return jax.shard_map(
        per_device,
        mesh=mesh,
        in_specs=placed,
        out_specs=(P(None, "shard"), P(None, "shard")),
        check_vma=False,
    )
```

profile of v0, /device:TPU:1, one launch (start us, length us, event | category | flops | bytes accessed | tf_op | source)
XLA Modules:
  0.0 292.6 jit_solution(13612801315061107417)
XLA Ops:
  7.2 1.0 convert.8
  9.5 0.9 reshape.89
  10.4 18.2 %all-to-all-start = ((bf16[64,2,1024]{2,1,0:T(2,128)(2,1)}), bf16[64,2,1024]{2,1,0:T(2,128)(2,1)S(1)}, u32[]{:S(2)}, u32[]{:S(2)}) async-start(bf16[64,2,1024]{2,1,0:T(2,128)(2,1)} %reshape.89), calls=%async_computation | async-start | bytes 524288 | tf_op jit(solution)/shard_map/all_to_all | solution.py:63
  28.7 1.0 reduce.5
  29.7 0.9 reshape.91
  30.6 20.2 %all-to-all-done = bf16[64,2,1024]{2,1,0:T(2,128)(2,1)S(1)} async-done(((bf16[64,2,1024]{2,1,0:T(2,128)(2,1)}), bf16[64,2,1024]{2,1,0:T(2,128)(2,1)S(1)}, u32[]{:S(2)}, u32[]{:S(2)}) %all-to-all-start) | async-done | bytes 262176 | tf_op jit(solution)/shard_map/all_to_all | solution.py:63
  50.8 4.2 %all-to-all-start.1 = ((bf16[64,2,2304]{2,1,0:T(2,128)(2,1)}), bf16[64,2,2304]{2,1,0:T(2,128)(2,1)S(1)}, u32[]{:S(2)}, u32[]{:S(2)}) async-start(bf16[64,2,2304]{2,1,0:T(2,128)(2,1)} %reshape.91), calls=%async_computation.1 | async-start | bytes 1179648 | tf_op jit(solution)/shard_map/all_to_all | solution.py:60
  55.3 33.4 %all-to-all-done.1 = bf16[64,2,2304]{2,1,0:T(2,128)(2,1)S(1)} async-done(((bf16[64,2,2304]{2,1,0:T(2,128)(2,1)}), bf16[64,2,2304]{2,1,0:T(2,128)(2,1)S(1)}, u32[]{:S(2)}, u32[]{:S(2)}) %all-to-all-start.1) | async-done | bytes 589856 | tf_op jit(solution)/shard_map/all_to_all | solution.py:60
  89.1 15.8 %conditional.1 = (bf16[64,4608]{1,0:T(8,128)(2,1)S(1)}, bf16[64,2048]{1,0:T(8,128)(2,1)S(1)}) conditional(s32[]{:T(128)} %convert_element_type.56, bf16[64,1,2048]{2,1,0:T(2,128)(2,1)S(1)} %reshape.90, bf16[64,1,4608]{2,1,0:T(2,128)(2,1)S(1)} %reshape.92), branch_computations={%region_0.0_spmd, %region_2.0_spmd} | conditional | flops 7224717312 | bytes 26214446 | solution.py:77
  89.3 0.9 fusion.8
  91.3 1.1 fusion.32
  92.7 1.1 convolution_add_fusion.9
  93.9 1.1 fusion.33
  95.3 1.1 convolution_add_fusion.8
  96.5 1.1 fusion.34
  98.0 1.1 convolution_add_fusion.7
  99.1 1.1 fusion.35
  100.6 1.1 convolution_add_fusion.6
  101.7 1.1 fusion.36
  103.2 1.2 fusion.7
  105.6 0.9 reshape.95
  106.5 6.6 %all-to-all-start.3 = ((bf16[64,2,1024]{2,1,0:T(2,128)(2,1)}), bf16[64,2,1024]{2,1,0:T(2,128)(2,1)S(1)}, u32[]{:S(2)}, u32[]{:S(2)}) async-start(bf16[64,2,1024]{2,1,0:T(2,128)(2,1)} %reshape.95), calls=%async_computation.3 | async-start | bytes 524288 | tf_op jit(solution)/shard_map/all_to_all | solution.py:82
  113.1 1.0 reduce.6
  114.1 0.9 reshape.93
  115.1 20.2 %all-to-all-done.3 = bf16[64,2,1024]{2,1,0:T(2,128)(2,1)S(1)} async-done(((bf16[64,2,1024]{2,1,0:T(2,128)(2,1)}), bf16[64,2,1024]{2,1,0:T(2,128)(2,1)S(1)}, u32[]{:S(2)}, u32[]{:S(2)}) %all-to-all-start.3) | async-done | bytes 262176 | tf_op jit(solution)/shard_map/all_to_all | solution.py:82
  135.3 4.2 %all-to-all-start.2 = ((bf16[64,2,2304]{2,1,0:T(2,128)(2,1)}), bf16[64,2,2304]{2,1,0:T(2,128)(2,1)S(1)}, u32[]{:S(2)}, u32[]{:S(2)}) async-start(bf16[64,2,2304]{2,1,0:T(2,128)(2,1)} %reshape.93), calls=%async_computation.2 | async-start | bytes 1179648 | tf_op jit(solution)/shard_map/all_to_all | solution.py:81
  141.2 32.0 %all-to-all-done.2 = bf16[64,2,2304]{2,1,0:T(2,128)(2,1)S(1)} async-done(((bf16[64,2,2304]{2,1,0:T(2,128)(2,1)}), bf16[64,2,2304]{2,1,0:T(2,128)(2,1)S(1)}, u32[]{:S(2)}, u32[]{:S(2)}) %all-to-all-start.2) | async-done | bytes 589856 | tf_op jit(solution)/shard_map/all_to_all | solution.py:81
  174.5 0.9 fusion.16
  175.4 31.3 %all-gather.5.cloned.1.call-done = bf16[256,2048]{1,0:T(8,128)(2,1)} async-done(((bf16[32,2048]{1,0:T(8,128)(2,1)}), bf16[256,2048]{1,0:T(8,128)(2,1)}) %all-gather.5.cloned.1.call-update) | async-done | bytes 1048592 | tf_op jit(solution)/shard_map/all_gather | solution.py:112
  206.6 74.9 %all-gather.3.cloned.1.call-done = bf16[256,4608]{1,0:T(8,128)(2,1)} async-done(((bf16[32,4608]{1,0:T(8,128)(2,1)}), bf16[256,4608]{1,0:T(8,128)(2,1)}) %all-gather.3.cloned.1.call-update) | async-done | bytes 2359312 | tf_op jit(solution)/shard_map/all_gather | solution.py:111
  281.6 3.2 %copy.34 = bf16[256,4608]{1,0:T(8,128)(2,1)} copy(bf16[256,4608]{1,0:T(8,128)(2,1)} %all-gather.3.cloned.1.call-done) | data formatting | bytes 4718592
  284.8 1.0 copy.35
  (41 shorter events, 7.9 us)
Async XLA Ops:
  7.2 21.4 %copy-start.1 = (f32[32,4608]{1,0:T(8,128)S(1)}, f32[32,4608]{1,0:T(8,128)}, u32[]{:S(2)}) copy-start(f32[32,4608]{1,0:T(8,128)} %param.8) | copy-start | bytes 1769476
  10.4 40.4 %all-to-all-start = ((bf16[64,2,1024]{2,1,0:T(2,128)(2,1)}), bf16[64,2,1024]{2,1,0:T(2,128)(2,1)S(1)}, u32[]{:S(2)}, u32[]{:S(2)}) async-start(bf16[64,2,1024]{2,1,0:T(2,128)(2,1)} %reshape.89), calls=%async_computation | async-start | bytes 524288 | tf_op jit(solution)/shard_map/all_to_all | solution.py:63
  50.8 37.8 %all-to-all-start.1 = ((bf16[64,2,2304]{2,1,0:T(2,128)(2,1)}), bf16[64,2,2304]{2,1,0:T(2,128)(2,1)S(1)}, u32[]{:S(2)}, u32[]{:S(2)}) async-start(bf16[64,2,2304]{2,1,0:T(2,128)(2,1)} %reshape.91), calls=%async_computation.1 | async-start | bytes 1179648 | tf_op jit(solution)/shard_map/all_to_all | solution.py:60
  106.5 28.8 %all-to-all-start.3 = ((bf16[64,2,1024]{2,1,0:T(2,128)(2,1)}), bf16[64,2,1024]{2,1,0:T(2,128)(2,1)S(1)}, u32[]{:S(2)}, u32[]{:S(2)}) async-start(bf16[64,2,1024]{2,1,0:T(2,128)(2,1)} %reshape.95), calls=%async_computation.3 | async-start | bytes 524288 | tf_op jit(solution)/shard_map/all_to_all | solution.py:82
  114.1 25.5 %copy-start.4 = (f32[32]{0:T(128)S(1)}, f32[32]{0:T(128)}, u32[]{:S(2)}) copy-start(f32[32]{0:T(128)} %param.13) | copy-start | bytes 388
  114.1 25.5 %copy-start.5 = (s32[32]{0:T(128)S(1)}, s32[32]{0:T(128)}, u32[]{:S(2)}) copy-start(s32[32]{0:T(128)} %param.12) | copy-start | bytes 388
  115.1 25.2 %copy-start.3 = (bf16[32,2048]{1,0:T(8,128)(2,1)S(1)}, bf16[32,2048]{1,0:T(8,128)(2,1)}, u32[]{:S(2)}) copy-start(bf16[32,2048]{1,0:T(8,128)(2,1)} %param.11) | copy-start | bytes 393220
  135.3 37.8 %all-to-all-start.2 = ((bf16[64,2,2304]{2,1,0:T(2,128)(2,1)}), bf16[64,2,2304]{2,1,0:T(2,128)(2,1)S(1)}, u32[]{:S(2)}, u32[]{:S(2)}) async-start(bf16[64,2,2304]{2,1,0:T(2,128)(2,1)} %reshape.93), calls=%async_computation.2 | async-start | bytes 1179648 | tf_op jit(solution)/shard_map/all_to_all | solution.py:81
  139.5 67.1 %all-gather.5.cloned.1.call-start = ((), (), s32[]{:S(2)}) async-start(), calls=%async_computation.5 | async-start | bytes 1179648 | tf_op jit(solution)/shard_map/all_gather | solution.py:112
  141.1 33.4 %copy-start.2 = (bf16[32,4608]{1,0:T(8,128)(2,1)S(1)}, bf16[32,4608]{1,0:T(8,128)(2,1)}, u32[]{:S(2)}) copy-start(bf16[32,4608]{1,0:T(8,128)(2,1)} %param.10) | copy-start | bytes 884740
  141.1 140.5 %all-gather.3.cloned.1.call-start = ((), (), s32[]{:S(2)}) async-start(), calls=%async_computation.4 | async-start | bytes 2654208 | tf_op jit(solution)/shard_map/all_gather | solution.py:111
  206.6 78.2 %copy-start = (bf16[256,2048]{1,0:T(8,128)(2,1)S(1)}, bf16[256,2048]{1,0:T(8,128)(2,1)}, u32[]{:S(2)}) copy-start(bf16[256,2048]{1,0:T(8,128)(2,1)} %all-gather.5.cloned.1.call-done) | copy-start | bytes 3145732
Sparse Core Ops, SparseCore 0:
  144.2 62.4 all-gather.4
  210.4 71.1 all-gather.2
where the time goes:
time: 293 us
  waiting for transfers between devices  212 us (72%)
  starting transfers between devices  33.2 us (11%)
  between operations  14.3 us (5%)
  matrix products  13 us (4%)
  local copies, waits for them, and re-layouts  10.5 us (4%)
  other arithmetic  8.45 us (3%)
    all_gather x1, waiting for transfers between devices, per_device(): lax.all_gather(query_fresh.astype(jnp.bfloat16), 'fsdp', axis=0, tiled=True)  74.9 us
    all_to_all x1, waiting for transfers between devices, per_device(): lax.all_to_all(query_send.astype(jnp.bfloat16), 'shard', split_axis=0, co...  33.4 us
    all_to_all x1, waiting for transfers between devices, per_device(): lax.all_to_all(query_done, 'shard', split_axis=0, concat_axis=0, tiled=True)  32 us
    all_gather x1, waiting for transfers between devices, per_device(): lax.all_gather(key_value_fresh.astype(jnp.bfloat16), 'fsdp', axis=0, tile...  31.3 us
    all_to_all x1, waiting for transfers between devices, per_device(): lax.all_to_all(keyval_done, 'shard', split_axis=0, concat_axis=0, tiled=T...  20.2 us
    all_to_all x1, waiting for transfers between devices, per_device(): lax.all_to_all(keyval_send.astype(jnp.bfloat16), 'shard', split_axis=0, c...  20.2 us
    all_to_all x1, starting transfers between devices, per_device(): lax.all_to_all(keyval_send.astype(jnp.bfloat16), 'shard', split_axis=0, c...  18.2 us
    unnamed x22, local copies, waits for them, and re-layouts  9.33 us
  transfers between devices with their start and end apart: 6, of which 6 were waited for; matrix products, arithmetic and copies ran while one was open for 3% of the time, Pallas kernels for 0%

commit v1 on v0

v1 whole, which is shorter than its diff:
```python
import functools
import math
from types import SimpleNamespace

import jax
import jax.numpy as jnp
from jax import lax
from jax.experimental import pallas as pl
from jax.experimental.pallas import tpu as pltpu
from jax.sharding import PartitionSpec as P

COEF_A = 3.4445
COEF_B = -4.775
COEF_C = 2.0315
CLIP_TAU = 100.0
LEARNING_RATE = 0.5
DECAY_WEIGHT = 0.1
NS_ITERS = 5
PLAIN = 128

F32 = jnp.float32
BF16 = jnp.bfloat16
Z = 16
LANE = 128
X_RING = 4
MESH = pl.DeviceIdType.MESH


def make_kind(name, rows, rank, chunks):
    slabs = rank // LANE
    per_chunk = slabs // chunks
    sources = 4 * rows
    return SimpleNamespace(
        name=name,
        rows=rows,
        rank=rank,
        chunks=chunks,
        slabs=slabs,
        per_chunk=per_chunk,
        sources=sources,
        message=sources * per_chunk,
        size=Z * sources,
        piece=rows * rank,
        strip=rows * per_chunk * LANE,
        span=per_chunk * LANE,
        back_rows=rows // chunks,
    )


QUERY = make_kind("q", 3, 1536, 3)
KEYVAL = make_kind("kv", 4, 512, 2)
KINDS = (QUERY, KEYVAL)


def scratch_of(kind):
    g = kind.chunks
    dma = pltpu.SemaphoreType.DMA
    return dict(
        raw=pltpu.VMEM((32, kind.piece), F32),
        mom=pltpu.VMEM((g, 32, kind.strip), BF16),
        gather=pltpu.VMEM((g, 4, 16, kind.strip), BF16),
        weights=pltpu.VMEM((4, 16, kind.piece), BF16),
        turn=pltpu.VMEM((Z * kind.message, LANE), F32),
        out_z=pltpu.VMEM((g, Z * kind.message, LANE), BF16),
        in_z=pltpu.VMEM((g, Z * kind.message, LANE), BF16),
        back_out=pltpu.VMEM((g, Z * kind.message, LANE), BF16),
        back_in=pltpu.VMEM((g, Z * kind.message, LANE), BF16),
        matrix=pltpu.VMEM((kind.size, kind.rank), BF16),
        strips=pltpu.VMEM((g, 4, 16, kind.strip), BF16),
        r_raw=dma((1,)),
        s_gather=dma((g,)),
        r_gather=dma((g,)),
        s_weights=dma((1,)),
        r_weights=dma((1,)),
        s_z=dma((g,)),
        r_z=dma((g,)),
        s_back=dma((g,)),
        r_back=dma((g,)),
        s_y=dma((g,)),
        r_y=dma((g,)),
        s_x=dma((g,)),
        r_x=dma((g, 2)),
        r_relay=dma((g, 2)),
    )


NAMES = tuple(scratch_of(QUERY))


def split(value):
    high = value.astype(BF16)
    return high, (value - high.astype(F32)).astype(BF16)


def dot(left, right):
    return jnp.dot(left, right, preferred_element_type=F32)


def product(left, right):
    return dot(left[0], right[0]) + (dot(left[0], right[1]) + dot(left[1], right[0]))


def identity(size):
    first = lax.broadcasted_iota(jnp.int32, (size, size), 0)
    second = lax.broadcasted_iota(jnp.int32, (size, size), 1)
    return first == second


def newton_schulz(gram, size):
    diagonal = identity(size)
    square = jnp.sum(jnp.where(diagonal, gram, 0.0), axis=(0, 1), keepdims=True)
    inverse = 1.0 / (jnp.sqrt(square) + 1e-07)
    a = (gram * inverse) * inverse
    total = None
    for step in range(NS_ITERS):
        a_parts = split(a)
        poly = COEF_B * a + COEF_C * product(a_parts, a_parts)
        poly = jnp.where(diagonal, poly + COEF_A, poly)
        parts = split(poly)
        total = poly if total is None else product(parts, split(total))
        if step < NS_ITERS - 1:
            a = product(parts, split(product(parts, a_parts)))
    return total * inverse


def kernel(q_mom, kv_mom, q_weights, kv_weights, flags_in, logit_in, q_out, kv_out, *scratch):
    flags, logit, small_sems, *scratch = scratch
    fsdp = lax.axis_index("fsdp")
    shard = lax.axis_index("shard")
    y_hi, x = fsdp // X_RING, fsdp % X_RING
    y, z, core = shard // 32, (shard // 2) % Z, shard % 2
    me = y * 2 + core
    half = len(NAMES)
    q = SimpleNamespace(
        k=QUERY, m=q_mom, w=q_weights, out=q_out, **dict(zip(NAMES, scratch[:half]))
    )
    kv = SimpleNamespace(
        k=KEYVAL, m=kv_mom, w=kv_weights, out=kv_out, **dict(zip(NAMES, scratch[half:]))
    )
    both = (q, kv)

    def place(to_y, to_z, to_core):
        return to_y * 32 + to_z * 2 + to_core

    def send(source, target, s_sem, r_sem, device):
        pltpu.make_async_remote_copy(
            src_ref=source,
            dst_ref=target,
            send_sem=s_sem,
            recv_sem=r_sem,
            device_id=device,
            device_id_type=MESH,
        ).start()

    def keep(source, target, sem):
        pltpu.make_async_copy(source, target, sem).start()

    def wait(ref, sem):
        pltpu.make_async_copy(ref, ref, sem).wait()

    x_right = y_hi * X_RING + (x + 1) % X_RING
    x_left = y_hi * X_RING + (x + X_RING - 1) % X_RING
    other = (1 - y_hi) * X_RING + x

    for ref in both:
        pltpu.make_async_copy(ref.m, ref.raw, ref.r_raw.at[0]).start()
    small = ((flags_in, flags, small_sems.at[0]), (logit_in, logit, small_sems.at[1]))
    for source, target, sem in small:
        pltpu.make_async_copy(source, target, sem).start()
    barrier = pltpu.get_barrier_semaphore()

    def greet(to_fsdp, to_shard):
        pl.semaphore_signal(barrier, inc=1, device_id=(to_fsdp, to_shard), device_id_type=MESH)

    greet(fsdp, place(y, z, 1 - core))
    greet(fsdp, place(1 - y, z, core))
    greet(fsdp, place(1 - y, z, 1 - core))
    for to_y in (y, 1 - y):
        for to_core in (core, 1 - core):
            greet(other, place(to_y, z, to_core))
    greet(x_right, shard)
    greet(x_left, shard)

    def greet_z(step, carry):
        greet(fsdp, place(y, (z + step) % Z, core))
        return carry

    lax.fori_loop(1, Z, greet_z, 0)

    for ref in both:
        k = ref.k
        pltpu.make_async_copy(ref.m, ref.raw, ref.r_raw.at[0]).wait()
        for g in range(k.chunks):
            for r in range(k.rows):
                start = (r * k.slabs + g * k.per_chunk) * LANE
                ref.mom[g, :, r * k.span : (r + 1) * k.span] = ref.raw[
                    :, start : start + k.span
                ].astype(BF16)

    pl.semaphore_wait(barrier, 24)

    def to_group(ref, to_core, source, target, s_sem, r_sem):
        @pl.when(core == to_core)
        def _():
            keep(source(y), target, r_sem)

        @pl.when(core != to_core)
        def _():
            send(source(y), target, s_sem, r_sem, (fsdp, place(y, z, to_core)))

        send(source(1 - y), target, s_sem, r_sem, (fsdp, place(1 - y, z, to_core)))

    def rows16(to_y):
        return pl.ds(pl.multiple_of(to_y * 16, 16), 16)

    for g in range(max(k.chunks for k in KINDS)):
        for to_core, ref in enumerate(both):
            if g < ref.k.chunks:
                to_group(
                    ref,
                    to_core,
                    lambda to_y, ref=ref, g=g: ref.mom.at[g, rows16(to_y), :],
                    ref.gather.at[g, me],
                    ref.s_gather.at[g],
                    ref.r_gather.at[g],
                )
    for to_core, ref in enumerate(both):
        to_group(
            ref,
            to_core,
            lambda to_y, ref=ref: ref.w.at[rows16(to_y), :],
            ref.weights.at[me],
            ref.s_weights.at[0],
            ref.r_weights.at[0],
        )

    def z_send(k, source, target, s_sem, r_sem):
        def one(i, carry):
            far = jnp.where(i % 2 == 1, 8 - (i + 1) // 2, 8 + i // 2)
            to_z = (z + far) % Z
            start = pl.multiple_of(to_z * k.message, 16)
            send(
                source.at[pl.ds(start, k.message), :],
                target.at[pl.ds(pl.multiple_of(z * k.message, 16), k.message), :],
                s_sem,
                r_sem,
                (fsdp, place(y, to_z, core)),
            )
            return carry

        lax.fori_loop(0, Z - 1, one, 0)
        here = pl.ds(pl.multiple_of(z * k.message, 16), k.message)
        keep(source.at[here, :], target.at[here, :], r_sem)

    def every(k, offset):
        return pl.ds(offset, 16, stride=k.message)

    def exchange(ref):
        k = ref.k
        for g in range(k.chunks):
            wait(ref.gather.at[g], ref.r_gather.at[g])
            for s in range(4):
                for r in range(k.rows):
                    for c in range(k.per_chunk):
                        start = (r * k.per_chunk + c) * LANE
                        tile = ref.gather[g, s, :, start : start + LANE]
                        ref.turn[every(k, c * k.sources + r * 4 + s), :] = tile.astype(F32)
            ref.out_z[g] = ref.turn[...].astype(BF16)
            z_send(k, ref.out_z.at[g], ref.in_z.at[g], ref.s_z.at[g], ref.r_z.at[g])

    def orthogonalize(ref):
        k = ref.k
        gram = None
        for g in range(k.chunks):
            wait(ref.in_z.at[g], ref.r_z.at[g])
            ref.turn[...] = ref.in_z[g].astype(F32)
            for c in range(k.per_chunk):
                column = (g * k.per_chunk + c) * LANE
                for n in range(k.sources):
                    tile = ref.turn[every(k, c * k.sources + n), :]
                    ref.matrix[n * 16 : n * 16 + 16, column : column + LANE] = tile.astype(BF16)
            part = ref.matrix[:, g * k.span : (g + 1) * k.span]
            term = lax.dot_general(
                part, part, (((1,), (1,)), ((), ())), preferred_element_type=F32
            )
            gram = term if gram is None else gram + term
        high, low = split(newton_schulz(gram, k.size))
        for g in range(k.chunks):
            rows = k.back_rows * 4
            own = slice(g * rows * 16, (g + 1) * rows * 16)
            whole = ref.matrix[...]
            update = dot(high[own], whole) + dot(low[own], whole)
            for n in range(rows):
                for c in range(k.slabs):
                    ref.turn[every(k, n * k.slabs + c), :] = update[
                        n * 16 : n * 16 + 16, c * LANE : (c + 1) * LANE
                    ]
            ref.back_out[g] = ref.turn[...].astype(BF16)
            z_send(k, ref.back_out.at[g], ref.back_in.at[g], ref.s_back.at[g], ref.r_back.at[g])

    def scales():
        ratio = jnp.minimum(1.0, CLIP_TAU / logit[...])
        eta_row = jnp.where(flags[...] > 0, ratio, 1.0)
        spread = jnp.where(identity(32), jnp.broadcast_to(eta_row, (32, 32)), 0.0)
        column = jnp.sum(spread, axis=1, keepdims=True)
        eta = jnp.where(y == 0, column[:16], column[16:])
        return jnp.broadcast_to(eta, (16, LANE)), jnp.broadcast_to(jnp.sqrt(eta), (16, LANE))

    def part(ref, g, start, count):
        rows = pl.ds(pl.multiple_of(start, 16), count)
        return ref.out.at[rows, g * ref.k.strip : (g + 1) * ref.k.strip]

    def renew(ref, g, eta, root):
        k = ref.k
        wait(ref.back_in.at[g], ref.r_back.at[g])
        ref.turn[...] = ref.back_in[g].astype(F32)
        tail = eta if k is QUERY else jnp.ones_like(eta)
        for r in range(k.back_rows):
            for s in range(4):
                row = ((s // 2) * 32 + z * 2 + s % 2) * k.rows + g * k.back_rows + r
                scale = jnp.where(row < PLAIN, root, tail)
                for c in range(k.slabs):
                    update = ref.turn[every(k, (r * 4 + s) * k.slabs + c), :]
                    start = (r * k.slabs + c) * LANE
                    column = g * k.strip + start
                    old = ref.weights[s, :, column : column + LANE].astype(F32)
                    fresh = scale * (
                        old * (1.0 - LEARNING_RATE * DECAY_WEIGHT)
                        - LEARNING_RATE * 0.2 * math.sqrt(k.rank) * update
                    )
                    ref.strips[g, s, :, start : start + LANE] = fresh.astype(BF16)
        mine = part(ref, g, fsdp * 32 + y * 16, 16)
        sems = ref.s_y.at[g], ref.r_y.at[g]
        for to_core in (core, 1 - core):
            strip = ref.strips.at[g, y * 2 + to_core]
            send(strip, mine, *sems, (other, place(y, z, to_core)))
            strip = ref.strips.at[g, (1 - y) * 2 + to_core]
            send(strip, mine, *sems, (fsdp, place(1 - y, z, to_core)))
            send(strip, mine, *sems, (other, place(1 - y, z, to_core)))
        send(ref.strips.at[g, y * 2 + 1 - core], mine, *sems, (fsdp, place(y, z, 1 - core)))
        keep(ref.strips.at[g, me], mine, ref.r_y.at[g])

    def block(ref, g, from_y_hi, from_x):
        start = (from_y_hi * X_RING + from_x) * 32
        return part(ref, g, start, 32)

    def along_x(ref, g):
        wait(part(ref, g, 0, 64), ref.r_y.at[g])
        for h in range(2):
            rows = block(ref, g, h, x)
            send(rows, rows, ref.s_x.at[g], ref.r_x.at[g, 0], (x_right, shard))
            send(rows, rows, ref.s_x.at[g], ref.r_x.at[g, 1], (x_left, shard))

    def relay(ref, g):
        wait(part(ref, g, 0, 64), ref.r_x.at[g, 0])
        rows = block(ref, g, 0, (x + X_RING - 1) % X_RING)
        send(rows, rows, ref.s_x.at[g], ref.r_relay.at[g, 0], (x_right, shard))
        wait(part(ref, g, 0, 64), ref.r_x.at[g, 1])
        rows = block(ref, g, 1, (x + 1) % X_RING)
        send(rows, rows, ref.s_x.at[g], ref.r_relay.at[g, 1], (x_left, shard))

    def run(ref):
        k = ref.k
        exchange(ref)
        orthogonalize(ref)
        for source, target, sem in small:
            pltpu.make_async_copy(source, target, sem).wait()
        eta, root = scales()
        wait(ref.weights, ref.r_weights.at[0])
        if k is KEYVAL:
            renew(kv, 0, eta, root)
            renew(kv, 1, eta, root)
        along_x(kv, 0)
        along_x(kv, 1)
        for g in range(3):
            if k is QUERY:
                renew(q, g, eta, root)
            if g == 0:
                relay(kv, 0)
                relay(kv, 1)
            along_x(q, g)
            if g > 0:
                relay(q, g - 1)
        relay(q, 2)
        for g in range(k.chunks):
            wait(part(ref, g, 0, 112), ref.s_y.at[g])
            most = pl.ds(0, (Z - 1) * k.message)
            wait(ref.out_z.at[g, most, :], ref.s_z.at[g])
            wait(ref.back_out.at[g, most, :], ref.s_back.at[g])
            wait(ref.mom.at[g, pl.ds(0, 16), :], ref.s_gather.at[g])
        wait(ref.weights.at[0], ref.s_weights.at[0])
        away = kv if ref is q else q
        for g in range(away.k.chunks):
            wait(away.mom.at[g], away.s_gather.at[g])
        wait(away.weights.at[pl.ds(0, 2)], away.s_weights.at[0])

    pl.when(core == 0)(lambda: run(q))
    pl.when(core == 1)(lambda: run(kv))

    for ref in both:
        for g in range(ref.k.chunks):
            wait(part(ref, g, 0, 32), ref.r_relay.at[g, 0])
            wait(part(ref, g, 0, 32), ref.r_relay.at[g, 1])
            wait(part(ref, g, 0, 192), ref.s_x.at[g])


def per_device(
    query_momentum, key_value_momentum, query_blocks, key_value_blocks, clip_flags, logit_max
):
    hbm = pl.BlockSpec(memory_space=pltpu.HBM)
    anywhere = pl.BlockSpec(memory_space=pl.ANY)
    scratch = [
        pltpu.VMEM((1, 32), jnp.int32),
        pltpu.VMEM((1, 32), F32),
        pltpu.SemaphoreType.DMA((2,)),
    ]
    for k in KINDS:
        scratch += list(scratch_of(k).values())
    return pl.pallas_call(
        kernel,
        name="muon",
        out_shape=tuple(pltpu.VMEM((256, k.piece), BF16) for k in KINDS),
        in_specs=[hbm] * 6,
        out_specs=(anywhere, anywhere),
        scratch_shapes=scratch,
        compiler_params=pltpu.CompilerParams(
            collective_id=0, has_side_effects=True, vmem_limit_bytes=60 * 1024 * 1024
        ),
    )(
        query_momentum,
        key_value_momentum,
        query_blocks,
        key_value_blocks,
        clip_flags.reshape(1, 32),
        logit_max.reshape(1, 32),
    )


def solution(mesh):
    placed = (
        P("fsdp", "shard"),
        P("fsdp", "shard"),
        P("fsdp", "shard"),
        P("fsdp", "shard"),
        P("fsdp"),
        P("fsdp"),
    )
    return jax.shard_map(
        per_device,
        mesh=mesh,
        in_specs=placed,
        out_specs=(P(None, "shard"), P(None, "shard")),
        check_vma=False,
    )
```

time: 293 us -> 87.5 us (0.30)
  waiting for transfers between devices: 212 us -> 0 us
  Pallas kernels: 0 us -> 84.3 us
  starting transfers between devices: 33.2 us -> 0 us
  between operations: 14.3 us -> 0.64 us
  matrix products: 13 us -> 0 us
  other arithmetic: 8.45 us -> 0 us
  local copies, waits for them, and re-layouts: 10.5 us -> 2.38 us
    all_gather x2 -> x0, waiting for transfers between devices: 106 us -> none  [the longest x1 74.9 us: per_device(): lax.all_gather(query_fresh.astype(jnp.bfloat16), 'fsdp', axis=0, tiled=True)]
    all_to_all x4 -> x0, waiting for transfers between devices: 106 us -> none  [the longest x1 33.4 us: per_device(): lax.all_to_all(query_send.astype(jnp.bfloat16), 'shard', split_axis=0, co...]
    pallas_call x0 -> x1, Pallas kernels: none -> 84.3 us  [per_device(): pl.pallas_call(kernel, name='muon', out_shape=tuple((pltpu.VMEM((256, k.p...]
    all_to_all x4 -> x0, starting transfers between devices: 33.1 us -> none  [the longest x1 18.2 us: per_device(): lax.all_to_all(keyval_send.astype(jnp.bfloat16), 'shard', split_axis=0, c...]
    dot_general x15 -> x0, matrix products: 13 us -> none  [the longest x5 5.76 us: make_orthogonal(): jnp.dot(polynomial, iterate, precision=lax.Precision.HIGHEST)]
    unnamed x22 -> x2, local copies, waits for them, and re-layouts: 9.33 us -> 2.38 us
    all_to_all x4 -> x0, other arithmetic: 3.53 us -> none  [the longest x1 1.02 us: per_device(): lax.all_to_all(query_send.astype(jnp.bfloat16), 'shard', split_axis=0, co...]
  transfers between devices with their start and end apart: 6 -> 0, of which waited for: 6 -> 0; matrix products, arithmetic and copies ran while one was open for 3% -> 0% of each run, Pallas kernels for 0% -> 0%
where the time goes in v1:
time: 87.5 us; the launch traced here: 87.4 us
  Pallas kernels  84.3 us (96%)
  local copies, waits for them, and re-layouts  2.38 us (3%)
    pallas_call x1, Pallas kernels, per_device(): pl.pallas_call(kernel, name='muon', out_shape=tuple((pltpu.VMEM((256, k.p...  84.3 us
    unnamed x2, local copies, waits for them, and re-layouts  2.38 us

profile of v1, /device:TPU:1, one launch (start us, length us, event | category | flops | bytes accessed | tf_op | source)
XLA Modules:
  0.0 87.4 jit_solution(7443577674942502972)
XLA Ops:
  0.6 84.3 %muon.1 = (bf16[256,4608]{1,0:T(8,128)(2,1)S(1)}, bf16[256,2048]{1,0:T(8,128)(2,1)S(1)}) custom-call(f32[32,4608]{1,0:T(8,128)} %q_mom.1, f32[32,2048]{1,0:T(8,128)} %kv_mom.1, bf16[32,4608]{1,0:T(8,128)(2,1)} %q_weights.1, bf16[32,2048]{1,0:T(8,128)(2,1)} %kv_weights.1, s32[1,32]{1,0:T(1,128)} %bitcast.2, f32[1,32]{1,0:T(1,128)} %bitcast.3), custom_call_target="tpu_custom_call" | custom-call | tf_op jit(solution)/shard_map/muon/pallas_call | solution.py:419
  85.0 1.4 %copy.10 = bf16[256,4608]{1,0:T(8,128)(2,1)} copy(bf16[256,4608]{1,0:T(8,128)(2,1)S(1)} %get-tuple-element.2) | data formatting | bytes 4718592
  86.4 1.0 %copy.11 = bf16[256,2048]{1,0:T(8,128)(2,1)} copy(bf16[256,2048]{1,0:T(8,128)(2,1)S(1)} %get-tuple-element.3) | data formatting | bytes 2097152

commit v2 on v1

--- a/solution.py
+++ b/solution.py
@@ -26,7 +26,7 @@
 MESH = pl.DeviceIdType.MESH
 
 
-def make_kind(name, rows, rank, chunks):
+def make_kind(name, rows, rank, chunks, back):
     slabs = rank // LANE
     per_chunk = slabs // chunks
     sources = 4 * rows
@@ -43,17 +43,19 @@
         piece=rows * rank,
         strip=rows * per_chunk * LANE,
         span=per_chunk * LANE,
-        back_rows=rows // chunks,
-    )
-
-
-QUERY = make_kind("q", 3, 1536, 3)
-KEYVAL = make_kind("kv", 4, 512, 2)
+        back=tuple((sum(back[:i]), n) for i, n in enumerate(back)),
+    )
+
+
+UNIT = 512
+QUERY = make_kind("q", 3, 1536, 3, (3, 3, 2, 1))
+KEYVAL = make_kind("kv", 4, 512, 2, (2, 2))
 KINDS = (QUERY, KEYVAL)
 
 
 def scratch_of(kind):
-    g = kind.chunks
+    g, b = kind.chunks, len(kind.back)
+    back_size = Z * 4 * kind.piece // LANE
     dma = pltpu.SemaphoreType.DMA
     return dict(
         raw=pltpu.VMEM((32, kind.piece), F32),
@@ -63,24 +65,29 @@
         turn=pltpu.VMEM((Z * kind.message, LANE), F32),
         out_z=pltpu.VMEM((g, Z * kind.message, LANE), BF16),
         in_z=pltpu.VMEM((g, Z * kind.message, LANE), BF16),
-        back_out=pltpu.VMEM((g, Z * kind.message, LANE), BF16),
-        back_in=pltpu.VMEM((g, Z * kind.message, LANE), BF16),
+        back_out=pltpu.VMEM((back_size, LANE), BF16),
+        back_in=pltpu.VMEM((back_size, LANE), BF16),
         matrix=pltpu.VMEM((kind.size, kind.rank), BF16),
-        strips=pltpu.VMEM((g, 4, 16, kind.strip), BF16),
+        strips=pltpu.VMEM((4, 16, kind.piece), BF16),
         r_raw=dma((1,)),
+        cross=pltpu.VMEM((2, 2, 16, kind.piece), BF16),
+        s_cross=dma((b,)),
+        r_cross=dma((b, 2)),
+        s_pass=dma((b,)),
+        r_pass=dma((b, 2)),
         s_gather=dma((g,)),
         r_gather=dma((g,)),
         s_weights=dma((1,)),
         r_weights=dma((1,)),
         s_z=dma((g,)),
         r_z=dma((g,)),
-        s_back=dma((g,)),
-        r_back=dma((g,)),
-        s_y=dma((g,)),
-        r_y=dma((g,)),
-        s_x=dma((g,)),
-        r_x=dma((g, 2)),
-        r_relay=dma((g, 2)),
+        s_back=dma((b,)),
+        r_back=dma((b,)),
+        s_y=dma((b,)),
+        r_y=dma((b,)),
+        s_x=dma((b,)),
+        r_x=dma((b, 2)),
+        r_relay=dma((b, 2)),
     )
 
 
@@ -96,8 +103,17 @@
     return jnp.dot(left, right, preferred_element_type=F32)
 
 
-def product(left, right):
-    return dot(left[0], right[0]) + (dot(left[0], right[1]) + dot(left[1], right[0]))
+def products(lefts, right):
+    high, low = right
+    size = high.shape[0]
+    by_high = dot(jnp.concatenate([term for left in lefts for term in left], axis=0), high)
+    by_low = dot(jnp.concatenate([left[0] for left in lefts], axis=0), low)
+    results = []
+    for i in range(len(lefts)):
+        first, second = 2 * i * size, (2 * i + 1) * size
+        small = by_high[second : second + size] + by_low[i * size : (i + 1) * size]
+        results.append(by_high[first : first + size] + small)
+    return results
 
 
 def identity(size):
@@ -114,12 +130,16 @@
     total = None
     for step in range(NS_ITERS):
         a_parts = split(a)
-        poly = COEF_B * a + COEF_C * product(a_parts, a_parts)
+        poly = COEF_B * a + COEF_C * products([a_parts], a_parts)[0]
         poly = jnp.where(diagonal, poly + COEF_A, poly)
         parts = split(poly)
-        total = poly if total is None else product(parts, split(total))
-        if step < NS_ITERS - 1:
-            a = product(parts, split(product(parts, a_parts)))
+        lefts = [a_parts] if step < NS_ITERS - 1 else []
+        if total is not None:
+            lefts.append(split(total))
+        results = products(lefts, parts)
+        total = poly if total is None else results.pop()
+        if results:
+            a = products([split(results[0])], parts)[0]
     return total * inverse
 
 
@@ -213,35 +233,43 @@
     def rows16(to_y):
         return pl.ds(pl.multiple_of(to_y * 16, 16), 16)
 
-    for g in range(max(k.chunks for k in KINDS)):
+    def gather(g):
         for to_core, ref in enumerate(both):
             if g < ref.k.chunks:
                 to_group(
                     ref,
                     to_core,
-                    lambda to_y, ref=ref, g=g: ref.mom.at[g, rows16(to_y), :],
+                    lambda to_y, ref=ref: ref.mom.at[g, rows16(to_y), :],
                     ref.gather.at[g, me],
                     ref.s_gather.at[g],
                     ref.r_gather.at[g],
                 )
-    for to_core, ref in enumerate(both):
-        to_group(
-            ref,
-            to_core,
-            lambda to_y, ref=ref: ref.w.at[rows16(to_y), :],
-            ref.weights.at[me],
-            ref.s_weights.at[0],
-            ref.r_weights.at[0],
-        )
-
-    def z_send(k, source, target, s_sem, r_sem):
+
+    def gathered(own, g):
+        for ref in both:
+            if g < ref.k.chunks:
+                strips = ref.mom.at[g, pl.ds(0, 16), :] if ref is own else ref.mom.at[g]
+                wait(strips, ref.s_gather.at[g])
+
+    def send_weights():
+        for to_core, ref in enumerate(both):
+            to_group(
+                ref,
+                to_core,
+                lambda to_y, ref=ref: ref.w.at[rows16(to_y), :],
+                ref.weights.at[me],
+                ref.s_weights.at[0],
+                ref.r_weights.at[0],
+            )
+
+    def z_send(rows, source, target, s_sem, r_sem):
         def one(i, carry):
             far = jnp.where(i % 2 == 1, 8 - (i + 1) // 2, 8 + i // 2)
             to_z = (z + far) % Z
-            start = pl.multiple_of(to_z * k.message, 16)
+            start = pl.multiple_of(to_z * rows, 16)
             send(
-                source.at[pl.ds(start, k.message), :],
-                target.at[pl.ds(pl.multiple_of(z * k.message, 16), k.message), :],
+                source.at[pl.ds(start, rows), :],
+                target.at[pl.ds(pl.multiple_of(z * rows, 16), rows), :],
                 s_sem,
                 r_sem,
                 (fsdp, place(y, to_z, core)),
@@ -249,24 +277,31 @@
             return carry
 
         lax.fori_loop(0, Z - 1, one, 0)
-        here = pl.ds(pl.multiple_of(z * k.message, 16), k.message)
+        here = pl.ds(pl.multiple_of(z * rows, 16), rows)
         keep(source.at[here, :], target.at[here, :], r_sem)
 
-    def every(k, offset):
-        return pl.ds(offset, 16, stride=k.message)
+    def every(rows, offset):
+        return pl.ds(offset, 16, stride=rows)
 
     def exchange(ref):
         k = ref.k
-        for g in range(k.chunks):
+        rounds = max(kind.chunks for kind in KINDS)
+        gather(0)
+        for g in range(rounds):
+            gathered(ref, g)
+            if g + 1 < rounds:
+                gather(g + 1)
+            if g >= k.chunks:
+                continue
             wait(ref.gather.at[g], ref.r_gather.at[g])
             for s in range(4):
                 for r in range(k.rows):
                     for c in range(k.per_chunk):
                         start = (r * k.per_chunk + c) * LANE
                         tile = ref.gather[g, s, :, start : start + LANE]
-                        ref.turn[every(k, c * k.sources + r * 4 + s), :] = tile.astype(F32)
+                        ref.turn[every(k.message, c * k.sources + r * 4 + s), :] = tile.astype(F32)
             ref.out_z[g] = ref.turn[...].astype(BF16)
-            z_send(k, ref.out_z.at[g], ref.in_z.at[g], ref.s_z.at[g], ref.r_z.at[g])
+            z_send(k.message, ref.out_z.at[g], ref.in_z.at[g], ref.s_z.at[g], ref.r_z.at[g])
 
     def orthogonalize(ref):
         k = ref.k
@@ -277,26 +312,49 @@
             for c in range(k.per_chunk):
                 column = (g * k.per_chunk + c) * LANE
                 for n in range(k.sources):
-                    tile = ref.turn[every(k, c * k.sources + n), :]
+                    tile = ref.turn[every(k.message, c * k.sources + n), :]
                     ref.matrix[n * 16 : n * 16 + 16, column : column + LANE] = tile.astype(BF16)
             part = ref.matrix[:, g * k.span : (g + 1) * k.span]
             term = lax.dot_general(
                 part, part, (((1,), (1,)), ((), ())), preferred_element_type=F32
             )
             gram = term if gram is None else gram + term
-        high, low = split(newton_schulz(gram, k.size))
-        for g in range(k.chunks):
-            rows = k.back_rows * 4
-            own = slice(g * rows * 16, (g + 1) * rows * 16)
-            whole = ref.matrix[...]
-            update = dot(high[own], whole) + dot(low[own], whole)
-            for n in range(rows):
-                for c in range(k.slabs):
-                    ref.turn[every(k, n * k.slabs + c), :] = update[
+        return split(newton_schulz(gram, k.size))
+
+    def prepare(ref, terms, g):
+        k = ref.k
+        high, low = terms
+        first, units = k.back[g]
+        for i in range(units):
+            row, column = divmod((first + i) * UNIT, k.rank)
+            own = slice(row * 64, row * 64 + 64)
+            both_terms = jnp.concatenate([high[own], low[own]], axis=0)
+            both_terms = dot(both_terms, ref.matrix[:, column : column + UNIT])
+            update = both_terms[:64] + both_terms[64:]
+            for n in range(4):
+                for c in range(4):
+                    ref.turn[every(units * 16, i * 16 + n * 4 + c), :] = update[
                         n * 16 : n * 16 + 16, c * LANE : (c + 1) * LANE
                     ]
-            ref.back_out[g] = ref.turn[...].astype(BF16)
-            z_send(k, ref.back_out.at[g], ref.back_in.at[g], ref.s_back.at[g], ref.r_back.at[g])
+        ref.back_out[back_span(first, units), :] = ref.turn[: Z * units * 16].astype(BF16)
+
+    def start_back(ref, g):
+        first, units = ref.k.back[g]
+        span = back_span(first, units)
+        sems = ref.s_back.at[g], ref.r_back.at[g]
+        z_send(units * 16, ref.back_out.at[span, :], ref.back_in.at[span, :], *sems)
+
+    def left_back(ref, g):
+        units = ref.k.back[g][1]
+        wait(ref.back_out.at[pl.ds(0, (Z - 1) * 16 * units), :], ref.s_back.at[g])
+
+    def back_span(first, units):
+        return pl.ds(Z * 16 * first, Z * 16 * units)
+
+    sides = (
+        (x_right, lax.rem(x + X_RING - 1, X_RING)),
+        (x_left, lax.rem(x + 1, X_RING)),
+    )
 
     def scales():
         ratio = jnp.minimum(1.0, CLIP_TAU / logit[...])
@@ -308,100 +366,150 @@
 
     def part(ref, g, start, count):
         rows = pl.ds(pl.multiple_of(start, 16), count)
-        return ref.out.at[rows, g * ref.k.strip : (g + 1) * ref.k.strip]
+        return ref.out.at[rows, chunk_columns(ref, g)]
+
+    def chunk_columns(ref, g):
+        first, units = ref.k.back[g]
+        return slice(first * UNIT, (first + units) * UNIT)
 
     def renew(ref, g, eta, root):
         k = ref.k
-        wait(ref.back_in.at[g], ref.r_back.at[g])
-        ref.turn[...] = ref.back_in[g].astype(F32)
+        first, units = k.back[g]
+        span = back_span(first, units)
+        wait(ref.back_in.at[span, :], ref.r_back.at[g])
+        ref.turn[: Z * units * 16] = ref.back_in[span, :].astype(F32)
         tail = eta if k is QUERY else jnp.ones_like(eta)
-        for r in range(k.back_rows):
+        for i in range(units):
             for s in range(4):
-                row = ((s // 2) * 32 + z * 2 + s % 2) * k.rows + g * k.back_rows + r
+                row = (first + i) * UNIT // k.rank
+                row = ((s // 2) * 32 + z * 2 + s % 2) * k.rows + row
                 scale = jnp.where(row < PLAIN, root, tail)
-                for c in range(k.slabs):
-                    update = ref.turn[every(k, (r * 4 + s) * k.slabs + c), :]
-                    start = (r * k.slabs + c) * LANE
-                    column = g * k.strip + start
+                for c in range(4):
+                    update = ref.turn[every(units * 16, i * 16 + s * 4 + c), :]
+                    column = (first + i) * UNIT + c * LANE
                     old = ref.weights[s, :, column : column + LANE].astype(F32)
                     fresh = scale * (
                         old * (1.0 - LEARNING_RATE * DECAY_WEIGHT)
                         - LEARNING_RATE * 0.2 * math.sqrt(k.rank) * update
                     )
-                    ref.strips[g, s, :, start : start + LANE] = fresh.astype(BF16)
+                    ref.strips[s, :, column : column + LANE] = fresh.astype(BF16)
+        columns = chunk_columns(ref, g)
         mine = part(ref, g, fsdp * 32 + y * 16, 16)
+        pair = ref.strips.at[pl.ds(pl.multiple_of((1 - y) * 2, 2), 2), :, columns]
+        for side, (to_fsdp, _) in enumerate(sides):
+            target = ref.cross.at[side, :, :, columns]
+            send(pair, target, ref.s_cross.at[g], ref.r_cross.at[g, side], (to_fsdp, shard))
         sems = ref.s_y.at[g], ref.r_y.at[g]
         for to_core in (core, 1 - core):
-            strip = ref.strips.at[g, y * 2 + to_core]
+            strip = ref.strips.at[y * 2 + to_core, :, columns]
             send(strip, mine, *sems, (other, place(y, z, to_core)))
-            strip = ref.strips.at[g, (1 - y) * 2 + to_core]
+            strip = ref.strips.at[(1 - y) * 2 + to_core, :, columns]
             send(strip, mine, *sems, (fsdp, place(1 - y, z, to_core)))
             send(strip, mine, *sems, (other, place(1 - y, z, to_core)))
-        send(ref.strips.at[g, y * 2 + 1 - core], mine, *sems, (fsdp, place(y, z, 1 - core)))
-        keep(ref.strips.at[g, me], mine, ref.r_y.at[g])
-
-    def block(ref, g, from_y_hi, from_x):
-        start = (from_y_hi * X_RING + from_x) * 32
-        return part(ref, g, start, 32)
+        strip = ref.strips.at[y * 2 + 1 - core, :, columns]
+        send(strip, mine, *sems, (fsdp, place(y, z, 1 - core)))
+        keep(ref.strips.at[me, :, columns], mine, ref.r_y.at[g])
+
+    def pass_on(ref, g):
+        columns = chunk_columns(ref, g)
+        for side, (_, from_x) in enumerate(sides):
+            landed = ref.cross.at[side, :, :, columns]
+            wait(landed, ref.r_cross.at[g, side])
+            target = part(ref, g, (y_hi * X_RING + from_x) * 32 + y * 16, 16)
+            sems = ref.s_pass.at[g], ref.r_pass.at[g, side]
+            for to_core in range(2):
+                strip = ref.cross.at[side, to_core, :, columns]
+                for to_fsdp in (fsdp, other):
+                    send(strip, target, *sems, (to_fsdp, place(1 - y, z, to_core)))
 
     def along_x(ref, g):
         wait(part(ref, g, 0, 64), ref.r_y.at[g])
         for h in range(2):
-            rows = block(ref, g, h, x)
-            send(rows, rows, ref.s_x.at[g], ref.r_x.at[g, 0], (x_right, shard))
-            send(rows, rows, ref.s_x.at[g], ref.r_x.at[g, 1], (x_left, shard))
+            rows = part(ref, g, (h * X_RING + x) * 32 + y * 16, 16)
+            for side, (to_fsdp, _) in enumerate(sides):
+                send(rows, rows, ref.s_x.at[g], ref.r_x.at[g, side], (to_fsdp, shard))
 
     def relay(ref, g):
-        wait(part(ref, g, 0, 64), ref.r_x.at[g, 0])
-        rows = block(ref, g, 0, (x + X_RING - 1) % X_RING)
-        send(rows, rows, ref.s_x.at[g], ref.r_relay.at[g, 0], (x_right, shard))
-        wait(part(ref, g, 0, 64), ref.r_x.at[g, 1])
-        rows = block(ref, g, 1, (x + 1) % X_RING)
-        send(rows, rows, ref.s_x.at[g], ref.r_relay.at[g, 1], (x_left, shard))
+        for side, (to_fsdp, from_x) in enumerate(sides):
+            wait(part(ref, g, 0, 32), ref.r_x.at[g, side])
+            wait(part(ref, g, 0, 32), ref.r_pass.at[g, side])
+            rows = part(ref, g, (side * X_RING + from_x) * 32, 32)
+            send(rows, rows, ref.s_x.at[g], ref.r_relay.at[g, side], (to_fsdp, shard))
 
     def run(ref):
         k = ref.k
         exchange(ref)
-        orthogonalize(ref)
+        send_weights()
+        terms = orthogonalize(ref)
+        prepare(ref, terms, 0)
+        start_back(ref, 0)
+        prepare(ref, terms, 1)
         for source, target, sem in small:
             pltpu.make_async_copy(source, target, sem).wait()
         eta, root = scales()
         wait(ref.weights, ref.r_weights.at[0])
+        left_back(ref, 0)
+        start_back(ref, 1)
         if k is KEYVAL:
             renew(kv, 0, eta, root)
+            along_x(kv, 0)
+            pass_on(kv, 0)
+            left_back(kv, 1)
             renew(kv, 1, eta, root)
-        along_x(kv, 0)
-        along_x(kv, 1)
-        for g in range(3):
-            if k is QUERY:
-                renew(q, g, eta, root)
-            if g == 0:
-                relay(kv, 0)
-                relay(kv, 1)
-            along_x(q, g)
-            if g > 0:
-                relay(q, g - 1)
+            along_x(kv, 1)
+            pass_on(kv, 1)
+            relay(kv, 0)
+            along_x(q, 0)
+            relay(kv, 1)
+            along_x(q, 1)
+            relay(q, 0)
+        else:
+            prepare(q, terms, 2)
+            along_x(kv, 0)
+            renew(q, 0, eta, root)
+            along_x(kv, 1)
+            left_back(q, 1)
+            start_back(q, 2)
+            prepare(q, terms, 3)
+            pass_on(q, 0)
+            along_x(q, 0)
+            renew(q, 1, eta, root)
+            left_back(q, 2)
+            start_back(q, 3)
+            relay(kv, 0)
+            pass_on(q, 1)
+            renew(q, 2, eta, root)
+            along_x(q, 1)
+            left_back(q, 3)
+            renew(q, 3, eta, root)
+            relay(kv, 1)
+            pass_on(q, 2)
+            pass_on(q, 3)
+            relay(q, 0)
+        along_x(q, 2)
+        along_x(q, 3)
+        relay(q, 1)
         relay(q, 2)
+        relay(q, 3)
+        for g in range(len(k.back)):
+            wait(part(ref, g, 0, 112), ref.s_y.at[g])
+            wait(part(ref, g, 0, 64), ref.s_cross.at[g])
+            wait(part(ref, g, 0, 128), ref.s_pass.at[g])
         for g in range(k.chunks):
-            wait(part(ref, g, 0, 112), ref.s_y.at[g])
             most = pl.ds(0, (Z - 1) * k.message)
             wait(ref.out_z.at[g, most, :], ref.s_z.at[g])
-            wait(ref.back_out.at[g, most, :], ref.s_back.at[g])
-            wait(ref.mom.at[g, pl.ds(0, 16), :], ref.s_gather.at[g])
         wait(ref.weights.at[0], ref.s_weights.at[0])
         away = kv if ref is q else q
-        for g in range(away.k.chunks):
-            wait(away.mom.at[g], away.s_gather.at[g])
         wait(away.weights.at[pl.ds(0, 2)], away.s_weights.at[0])
 
     pl.when(core == 0)(lambda: run(q))
     pl.when(core == 1)(lambda: run(kv))
 
     for ref in both:
-        for g in range(ref.k.chunks):
+        for g in range(len(ref.k.back)):
             wait(part(ref, g, 0, 32), ref.r_relay.at[g, 0])
             wait(part(ref, g, 0, 32), ref.r_relay.at[g, 1])
-            wait(part(ref, g, 0, 192), ref.s_x.at[g])
+            wait(part(ref, g, 0, 128), ref.s_x.at[g])
 
 
 def per_device(

time: 87.5 us -> 87.6 us (level)
  no operation moved by 1% of the time
where the time goes in v2:
time: 87.6 us; the launch traced here: 86.6 us
  Pallas kernels  83.6 us (95%)
  local copies, waits for them, and re-layouts  2.38 us (3%)
    pallas_call x1, Pallas kernels, per_device(): pl.pallas_call(kernel, name='muon', out_shape=tuple((pltpu.VMEM((256, k.p...  83.6 us
    unnamed x2, local copies, waits for them, and re-layouts  2.38 us

profile of v2, /device:TPU:1, one launch (start us, length us, event | category | flops | bytes accessed | tf_op | source)
XLA Modules:
  0.0 86.6 jit_solution(3773895920227846780)
XLA Ops:
  0.6 83.6 %muon.1 = (bf16[256,4608]{1,0:T(8,128)(2,1)S(1)}, bf16[256,2048]{1,0:T(8,128)(2,1)S(1)}) custom-call(f32[32,4608]{1,0:T(8,128)} %q_mom.1, f32[32,2048]{1,0:T(8,128)} %kv_mom.1, bf16[32,4608]{1,0:T(8,128)(2,1)} %q_weights.1, bf16[32,2048]{1,0:T(8,128)(2,1)} %kv_weights.1, s32[1,32]{1,0:T(1,128)} %bitcast.2, f32[1,32]{1,0:T(1,128)} %bitcast.3), custom_call_target="tpu_custom_call" | custom-call | tf_op jit(solution)/shard_map/muon/pallas_call | solution.py:527
  84.2 1.4 %copy.10 = bf16[256,4608]{1,0:T(8,128)(2,1)} copy(bf16[256,4608]{1,0:T(8,128)(2,1)S(1)} %get-tuple-element.2) | data formatting | bytes 4718592
  85.6 1.0 %copy.11 = bf16[256,2048]{1,0:T(8,128)(2,1)} copy(bf16[256,2048]{1,0:T(8,128)(2,1)S(1)} %get-tuple-element.3) | data formatting | bytes 2097152

commit v3 on v2

--- a/solution.py
+++ b/solution.py
@@ -468,29 +468,30 @@
             along_x(kv, 0)
             renew(q, 0, eta, root)
             along_x(kv, 1)
+            relay(kv, 0)
             left_back(q, 1)
             start_back(q, 2)
-            prepare(q, terms, 3)
             pass_on(q, 0)
             along_x(q, 0)
+            prepare(q, terms, 3)
             renew(q, 1, eta, root)
+            relay(kv, 1)
             left_back(q, 2)
             start_back(q, 3)
-            relay(kv, 0)
             pass_on(q, 1)
             renew(q, 2, eta, root)
             along_x(q, 1)
-            left_back(q, 3)
             renew(q, 3, eta, root)
-            relay(kv, 1)
+            relay(q, 0)
             pass_on(q, 2)
             pass_on(q, 3)
-            relay(q, 0)
         along_x(q, 2)
         along_x(q, 3)
         relay(q, 1)
         relay(q, 2)
         relay(q, 3)
+        if k is QUERY:
+            left_back(q, 3)
         for g in range(len(k.back)):
             wait(part(ref, g, 0, 112), ref.s_y.at[g])
             wait(part(ref, g, 0, 64), ref.s_cross.at[g])

time: 87.6 us -> 86.7 us (0.990); the launches traced: 86.6 us -> 86.6 us
  no operation moved by 1% of the time
where the time goes in v3:
time: 86.7 us; the launch traced here: 86.6 us
  Pallas kernels  83.6 us (96%)
  local copies, waits for them, and re-layouts  2.38 us (3%)
    pallas_call x1, Pallas kernels, per_device(): pl.pallas_call(kernel, name='muon', out_shape=tuple((pltpu.VMEM((256, k.p...  83.6 us
    unnamed x2, local copies, waits for them, and re-layouts  2.38 us

profile of v3, /device:TPU:1, one launch (start us, length us, event | category | flops | bytes accessed | tf_op | source)
XLA Modules:
  0.0 86.6 jit_solution(13276174824393807917)
XLA Ops:
  0.6 83.6 %muon.1 = (bf16[256,4608]{1,0:T(8,128)(2,1)S(1)}, bf16[256,2048]{1,0:T(8,128)(2,1)S(1)}) custom-call(f32[32,4608]{1,0:T(8,128)} %q_mom.1, f32[32,2048]{1,0:T(8,128)} %kv_mom.1, bf16[32,4608]{1,0:T(8,128)(2,1)} %q_weights.1, bf16[32,2048]{1,0:T(8,128)(2,1)} %kv_weights.1, s32[1,32]{1,0:T(1,128)} %bitcast.2, f32[1,32]{1,0:T(1,128)} %bitcast.3), custom_call_target="tpu_custom_call" | custom-call | tf_op jit(solution)/shard_map/muon/pallas_call | solution.py:528
  84.2 1.4 %copy.10 = bf16[256,4608]{1,0:T(8,128)(2,1)} copy(bf16[256,4608]{1,0:T(8,128)(2,1)S(1)} %get-tuple-element.2) | data formatting | bytes 4718592
  85.6 1.0 %copy.11 = bf16[256,2048]{1,0:T(8,128)(2,1)} copy(bf16[256,2048]{1,0:T(8,128)(2,1)S(1)} %get-tuple-element.3) | data formatting | bytes 2097152

commit v4 on v3

--- a/solution.py
+++ b/solution.py
@@ -452,12 +452,11 @@
         start_back(ref, 1)
         if k is KEYVAL:
             renew(kv, 0, eta, root)
+            pass_on(kv, 0)
             along_x(kv, 0)
-            pass_on(kv, 0)
-            left_back(kv, 1)
             renew(kv, 1, eta, root)
+            pass_on(kv, 1)
             along_x(kv, 1)
-            pass_on(kv, 1)
             relay(kv, 0)
             along_x(q, 0)
             relay(kv, 1)
@@ -465,19 +464,18 @@
             relay(q, 0)
         else:
             prepare(q, terms, 2)
+            prepare(q, terms, 3)
             along_x(kv, 0)
             renew(q, 0, eta, root)
             along_x(kv, 1)
             relay(kv, 0)
             left_back(q, 1)
             start_back(q, 2)
+            start_back(q, 3)
             pass_on(q, 0)
             along_x(q, 0)
-            prepare(q, terms, 3)
             renew(q, 1, eta, root)
             relay(kv, 1)
-            left_back(q, 2)
-            start_back(q, 3)
             pass_on(q, 1)
             renew(q, 2, eta, root)
             along_x(q, 1)
@@ -490,8 +488,8 @@
         relay(q, 1)
         relay(q, 2)
         relay(q, 3)
-        if k is QUERY:
-            left_back(q, 3)
+        for g in range(2 if k is QUERY else 1, len(k.back)):
+            left_back(ref, g)
         for g in range(len(k.back)):
             wait(part(ref, g, 0, 112), ref.s_y.at[g])
             wait(part(ref, g, 0, 64), ref.s_cross.at[g])

time: 86.7 us -> 86.6 us (level)
  no operation moved by 1% of the time
where the time goes in v4:
time: 86.6 us; the launch traced here: 86.5 us
  Pallas kernels  83.4 us (96%)
  local copies, waits for them, and re-layouts  2.38 us (3%)
    pallas_call x1, Pallas kernels, per_device(): pl.pallas_call(kernel, name='muon', out_shape=tuple((pltpu.VMEM((256, k.p...  83.4 us
    unnamed x2, local copies, waits for them, and re-layouts  2.38 us

profile of v4, /device:TPU:1, one launch (start us, length us, event | category | flops | bytes accessed | tf_op | source)
XLA Modules:
  0.0 86.5 jit_solution(6826755346156768011)
XLA Ops:
  0.6 83.4 %muon.1 = (bf16[256,4608]{1,0:T(8,128)(2,1)S(1)}, bf16[256,2048]{1,0:T(8,128)(2,1)S(1)}) custom-call(f32[32,4608]{1,0:T(8,128)} %q_mom.1, f32[32,2048]{1,0:T(8,128)} %kv_mom.1, bf16[32,4608]{1,0:T(8,128)(2,1)} %q_weights.1, bf16[32,2048]{1,0:T(8,128)(2,1)} %kv_weights.1, s32[1,32]{1,0:T(1,128)} %bitcast.2, f32[1,32]{1,0:T(1,128)} %bitcast.3), custom_call_target="tpu_custom_call" | custom-call | tf_op jit(solution)/shard_map/muon/pallas_call | solution.py:526
  84.1 1.4 %copy.10 = bf16[256,4608]{1,0:T(8,128)(2,1)} copy(bf16[256,4608]{1,0:T(8,128)(2,1)S(1)} %get-tuple-element.2) | data formatting | bytes 4718592
  85.5 1.0 %copy.11 = bf16[256,2048]{1,0:T(8,128)(2,1)} copy(bf16[256,2048]{1,0:T(8,128)(2,1)S(1)} %get-tuple-element.3) | data formatting | bytes 2097152

commit v5 on v4

--- a/solution.py
+++ b/solution.py
@@ -103,17 +103,8 @@
     return jnp.dot(left, right, preferred_element_type=F32)
 
 
-def products(lefts, right):
-    high, low = right
-    size = high.shape[0]
-    by_high = dot(jnp.concatenate([term for left in lefts for term in left], axis=0), high)
-    by_low = dot(jnp.concatenate([left[0] for left in lefts], axis=0), low)
-    results = []
-    for i in range(len(lefts)):
-        first, second = 2 * i * size, (2 * i + 1) * size
-        small = by_high[second : second + size] + by_low[i * size : (i + 1) * size]
-        results.append(by_high[first : first + size] + small)
-    return results
+def product(left, right):
+    return dot(left[0], right[0]) + (dot(left[0], right[1]) + dot(left[1], right[0]))
 
 
 def identity(size):
@@ -130,16 +121,12 @@
     total = None
     for step in range(NS_ITERS):
         a_parts = split(a)
-        poly = COEF_B * a + COEF_C * products([a_parts], a_parts)[0]
+        poly = COEF_B * a + COEF_C * product(a_parts, a_parts)
         poly = jnp.where(diagonal, poly + COEF_A, poly)
         parts = split(poly)
-        lefts = [a_parts] if step < NS_ITERS - 1 else []
-        if total is not None:
-            lefts.append(split(total))
-        results = products(lefts, parts)
-        total = poly if total is None else results.pop()
-        if results:
-            a = products([split(results[0])], parts)[0]
+        total = poly if total is None else product(parts, split(total))
+        if step < NS_ITERS - 1:
+            a = product(parts, split(product(parts, a_parts)))
     return total * inverse
 
 

time: 86.6 us -> 86.1 us (level)
  no operation moved by 1% of the time
where the time goes in v5:
time: 86.1 us; the launch traced here: 85.9 us
  Pallas kernels  82.9 us (96%)
  local copies, waits for them, and re-layouts  2.38 us (3%)
    pallas_call x1, Pallas kernels, per_device(): pl.pallas_call(kernel, name='muon', out_shape=tuple((pltpu.VMEM((256, k.p...  82.9 us
    unnamed x2, local copies, waits for them, and re-layouts  2.38 us

profile of v5, /device:TPU:1, one launch (start us, length us, event | category | flops | bytes accessed | tf_op | source)
XLA Modules:
  0.0 85.9 jit_solution(11812018308930873714)
XLA Ops:
  0.6 82.9 %muon.1 = (bf16[256,4608]{1,0:T(8,128)(2,1)S(1)}, bf16[256,2048]{1,0:T(8,128)(2,1)S(1)}) custom-call(f32[32,4608]{1,0:T(8,128)} %q_mom.1, f32[32,2048]{1,0:T(8,128)} %kv_mom.1, bf16[32,4608]{1,0:T(8,128)(2,1)} %q_weights.1, bf16[32,2048]{1,0:T(8,128)(2,1)} %kv_weights.1, s32[1,32]{1,0:T(1,128)} %bitcast.2, f32[1,32]{1,0:T(1,128)} %bitcast.3), custom_call_target="tpu_custom_call" | custom-call | tf_op jit(solution)/shard_map/muon/pallas_call | solution.py:513
  83.5 1.4 %copy.10 = bf16[256,4608]{1,0:T(8,128)(2,1)} copy(bf16[256,4608]{1,0:T(8,128)(2,1)S(1)} %get-tuple-element.2) | data formatting | bytes 4718592
  85.0 1.0 %copy.11 = bf16[256,2048]{1,0:T(8,128)(2,1)} copy(bf16[256,2048]{1,0:T(8,128)(2,1)S(1)} %get-tuple-element.3) | data formatting | bytes 2097152

commit v6 on v5

--- a/solution.py
+++ b/solution.py
@@ -48,7 +48,7 @@
 
 
 UNIT = 512
-QUERY = make_kind("q", 3, 1536, 3, (3, 3, 2, 1))
+QUERY = make_kind("q", 3, 1536, 3, (2, 3, 3, 1))
 KEYVAL = make_kind("kv", 4, 512, 2, (2, 2))
 KINDS = (QUERY, KEYVAL)
 

time: 86.1 us -> 85.8 us (level)
  no operation moved by 1% of the time
where the time goes in v6:
time: 85.8 us; the launch traced here: 85.7 us
  Pallas kernels  82.7 us (96%)
  local copies, waits for them, and re-layouts  2.38 us (3%)
    pallas_call x1, Pallas kernels, per_device(): pl.pallas_call(kernel, name='muon', out_shape=tuple((pltpu.VMEM((256, k.p...  82.7 us
    unnamed x2, local copies, waits for them, and re-layouts  2.38 us

profile of v6, /device:TPU:1, one launch (start us, length us, event | category | flops | bytes accessed | tf_op | source)
XLA Modules:
  0.0 85.7 jit_solution(4528930758133466261)
XLA Ops:
  0.6 82.7 %muon.1 = (bf16[256,4608]{1,0:T(8,128)(2,1)S(1)}, bf16[256,2048]{1,0:T(8,128)(2,1)S(1)}) custom-call(f32[32,4608]{1,0:T(8,128)} %q_mom.1, f32[32,2048]{1,0:T(8,128)} %kv_mom.1, bf16[32,4608]{1,0:T(8,128)(2,1)} %q_weights.1, bf16[32,2048]{1,0:T(8,128)(2,1)} %kv_weights.1, s32[1,32]{1,0:T(1,128)} %bitcast.2, f32[1,32]{1,0:T(1,128)} %bitcast.3), custom_call_target="tpu_custom_call" | custom-call | tf_op jit(solution)/shard_map/muon/pallas_call | solution.py:513
  83.3 1.4 %copy.10 = bf16[256,4608]{1,0:T(8,128)(2,1)} copy(bf16[256,4608]{1,0:T(8,128)(2,1)S(1)} %get-tuple-element.2) | data formatting | bytes 4718592
  84.7 1.0 %copy.11 = bf16[256,2048]{1,0:T(8,128)(2,1)} copy(bf16[256,2048]{1,0:T(8,128)(2,1)S(1)} %get-tuple-element.3) | data formatting | bytes 2097152
